TPU v7x, 32 devices: a whole 2x2x4 slice. The times are simulated.
32 devices in a mesh: fsdp: 16 (over z, x, core), tp: 2 (over y).
Axes of the slice: x: 2, y: 2, z: 4, core: 2. Of those that a mesh axis runs over, the one named last changes fastest.
Arguments:
- inputs: bfloat16 [32, 736, 1152], P('fsdp', 'tp'), may hold values from -6 to 6
- w_qkv: bfloat16 [3, 1152, 1152], P(None, 'fsdp', 'tp'), may hold values from -0.25 to 0.25
- w_out: bfloat16 [1152, 1152], P('tp', 'fsdp'), may hold values from -0.75 to 0.75
- w_up: bfloat16 [1152, 4304], P('fsdp', 'tp'), may hold values from -0.1875 to 0.1875
- w_down: bfloat16 [4304, 1152], P('tp', 'fsdp'), may hold values from -0.09375 to 0.09375
- norm_gains: float32 [2, 1152], replicated, may hold values from 0.1 to 1.9
- biases: float32 [6, 1152], replicated, may hold values from -3 to 3
- up_bias: float32 [4304], replicated, may hold values from -3 to 3
- cotangent: bfloat16 [32, 736, 1152], P('fsdp', 'tp'), may hold values from -6 to 6
Outputs:
- outputs: bfloat16 [32, 736, 1152], P('fsdp', 'tp')
- input_grad: float32 [32, 736, 1152], P('fsdp', 'tp')
- w_qkv_grad: float32 [3, 1152, 1152], P(None, 'fsdp', 'tp')
- w_out_grad: float32 [1152, 1152], P('tp', 'fsdp')
- w_up_grad: float32 [1152, 4304], P('fsdp', 'tp')
- w_down_grad: float32 [4304, 1152], P('tp', 'fsdp')
- norm_gains_grad: float32 [2, 1152], replicated
- biases_grad: float32 [6, 1152], replicated
- up_bias_grad: float32 [4304], replicated
All inputs are finite; a program needn't handle non-finite values.
Results may differ from a plain program's by a relative error of at most 0.018.
The roundings to bfloat16 on the way count: a program that leaves them out, or rounds other values in their place, can miss the bound.
Values may be sent and summed in bfloat16 or wider, within the bound.
A program may use at most 192 MiB of HBM per device.

v0:
```python
import math
import jax
import jax.numpy as jnp
from jax import lax
from jax.sharding import PartitionSpec as P

HD = 72
VALID = 729
norm_eps = 1e-06
gelu_coef = math.sqrt(2.0 / math.pi)


def norm_forward(values, scale_row, shift_row):
    average = jnp.mean(values, axis=-1, keepdims=True)
    centred = values - average
    inv_std = lax.rsqrt(jnp.mean(centred * centred, axis=-1, keepdims=True) + norm_eps)
    normed = centred * inv_std
    return (normed * scale_row + shift_row, normed, inv_std)


def norm_backward(upstream, normed, inv_std, scale_row):
    scaled = upstream * scale_row
    back = inv_std * (
        scaled
        - jnp.mean(scaled, axis=-1, keepdims=True)
        - normed * jnp.mean(scaled * normed, axis=-1, keepdims=True)
    )
    return (back, jnp.sum(upstream * normed, axis=0), jnp.sum(upstream, axis=0))


def gelu_tanh(pre_act):
    return (
        0.5
        * pre_act
        * (1.0 + jnp.tanh(gelu_coef * (pre_act + 0.044715 * pre_act * pre_act * pre_act)))
    )


def gelu_slope(pre_act):
    tangent = jnp.tanh(gelu_coef * (pre_act + 0.044715 * pre_act * pre_act * pre_act))
    inner_slope = gelu_coef * (1.0 + 3.0 * 0.044715 * pre_act * pre_act)
    return 0.5 * (1.0 + tangent) + 0.5 * pre_act * (1.0 - tangent * tangent) * inner_slope


def masked_scores(queries, key_rows, positions):
    seq_len = queries.shape[0]
    head_count = queries.shape[1] // HD
    query_heads = queries.reshape(seq_len, head_count, HD)
    key_heads = key_rows.reshape(seq_len, head_count, HD)
    scores = jnp.einsum("qhe,khe->hqk", query_heads, key_heads, preferred_element_type=jnp.float32)
    scores = scores * (1.0 / math.sqrt(HD))
    visible = (positions < VALID)[None, None, :]
    return (jnp.where(visible, scores, -1e30), query_heads, key_heads)


def attend_forward(queries, key_rows, values, positions):
    seq_len = queries.shape[0]
    scores, query_heads, key_heads = masked_scores(queries, key_rows, positions)
    value_heads = values.reshape(seq_len, -1, HD)
    largest = jnp.max(scores, axis=-1, keepdims=True)
    powers = jnp.exp(scores - largest)
    summed = jnp.sum(powers, axis=-1, keepdims=True)
    attn_probs = (powers / summed).astype(jnp.bfloat16)
    mixed_out = jnp.einsum(
        "hqk,khe->qhe", attn_probs, value_heads, preferred_element_type=jnp.float32
    )
    log_totals = (largest + jnp.log(summed))[:, :, 0]
    return (mixed_out.reshape(seq_len, queries.shape[1]).astype(jnp.bfloat16), log_totals)


def attend_backward(queries, key_rows, values, log_totals, d_mixed, positions):
    seq_len = queries.shape[0]
    scores, query_heads, key_heads = masked_scores(queries, key_rows, positions)
    value_heads = values.reshape(seq_len, -1, HD)
    grad_heads = d_mixed.reshape(seq_len, -1, HD)
    probs_full = jnp.exp(scores - log_totals[:, :, None])
    d_probs = jnp.einsum(
        "qhe,khe->hqk", grad_heads, value_heads, preferred_element_type=jnp.float32
    )
    row_inner = jnp.sum(probs_full * d_probs, axis=-1, keepdims=True)
    d_scores = (probs_full * (d_probs - row_inner)).astype(jnp.bfloat16)
    d_values = jnp.einsum(
        "hqk,qhe->khe",
        probs_full.astype(jnp.bfloat16),
        grad_heads,
        preferred_element_type=jnp.float32,
    )
    scale_now = 1.0 / math.sqrt(HD)
    d_queries = (
        jnp.einsum("hqk,khe->qhe", d_scores, key_heads, preferred_element_type=jnp.float32)
        * scale_now
    )
    d_keys = (
        jnp.einsum("hqk,qhe->khe", d_scores, query_heads, preferred_element_type=jnp.float32)
        * scale_now
    )
    parts = [d_queries, d_keys, d_values]
    return jnp.concatenate(
        [part.reshape(seq_len, queries.shape[1]).astype(jnp.bfloat16) for part in parts], axis=1
    )


def dot(left, right, dims):
    return lax.dot_general(left, right, (dims, ((), ())), preferred_element_type=jnp.float32)


ROWS_COLS = ((1,), (0,))
ROWS_ROWS = ((1,), (1,))
COLS_COLS = ((0,), (0,))


def swap_halves(block):
    return lax.ppermute(block, "tp", [(0, 1), (1, 0)])


def gather_rows(block):
    if lax.axis_size("tp") == 2:
        return jnp.concatenate([block, swap_halves(block)], axis=0)
    return lax.all_gather(block, "tp", axis=0, tiled=True)


def scatter_dot(left, right, dims):
    if lax.axis_size("tp") == 2:
        half = left.shape[0] // 2
        away = swap_halves(dot(left[half:], right, dims).astype(jnp.bfloat16))
        return dot(left[:half], right, dims) + away.astype(jnp.float32)
    return lax.psum_scatter(
        dot(left, right, dims).astype(jnp.bfloat16), "tp", scatter_dimension=0, tiled=True
    ).astype(jnp.float32)


def gather_weight(shard):
    return lax.all_gather(shard, "fsdp", axis=0, tiled=True)


def scatter_weight(whole):
    return lax.psum_scatter(
        whole.astype(jnp.bfloat16), "fsdp", scatter_dimension=0, tiled=True
    ).astype(jnp.float32)


def per_device(inputs, w_qkv, w_out, w_up, w_down, norm_gains, biases, up_bias, cotangent):
    image_count, rows_here, width = inputs.shape
    images = range(image_count)
    local_cols = w_qkv.shape[2]
    unit_count = w_up.shape[1]
    shard_rows = w_qkv.shape[1]
    tp_index = lax.axis_index("tp")
    seq_len = rows_here * lax.axis_size("tp")
    col_start = tp_index * local_cols
    unit_start = tp_index * unit_count
    positions = lax.iota(jnp.int32, seq_len)
    if lax.axis_size("tp") == 2:
        positions = positions + tp_index * rows_here
        positions = jnp.where(positions >= seq_len, positions - seq_len, positions)
    qkv_all = gather_weight(w_qkv.transpose(1, 0, 2).reshape(shard_rows, 3 * local_cols))
    out_all = gather_weight(w_out.T)
    up_all = gather_weight(w_up)
    down_all = gather_weight(w_down.T)
    query_bias = lax.dynamic_slice_in_dim(biases[1], col_start, local_cols)
    value_bias = lax.dynamic_slice_in_dim(biases[2], col_start, local_cols)
    unit_bias = lax.dynamic_slice_in_dim(up_bias, unit_start, unit_count)
    qkv_bias = jnp.concatenate([query_bias, jnp.zeros_like(query_bias), value_bias])
    residual = [inputs[i].astype(jnp.float32) for i in images]
    first = [norm_forward(residual[i], norm_gains[0], biases[0]) for i in images]
    gathered_one = [gather_rows(first[i][0].astype(jnp.bfloat16)) for i in images]
    grad_rows = [gather_rows(cotangent[i]) for i in images]
    saved, mixed, middle, second, gathered_two = ([], [], [], [], [])
    for i in images:
        projected = (dot(gathered_one[i], qkv_all, ROWS_COLS) + qkv_bias).astype(jnp.bfloat16)
        queries, key_rows, values = (
            projected[:, c * local_cols : (c + 1) * local_cols] for c in range(3)
        )
        mixed_out, log_totals = attend_forward(queries, key_rows, values, positions)
        saved.append((queries, key_rows, values, log_totals))
        mixed.append(mixed_out)
        middle.append(residual[i] + scatter_dot(mixed_out, out_all, ROWS_ROWS) + biases[3])
        second.append(norm_forward(middle[i], norm_gains[1], biases[4]))
        gathered_two.append(gather_rows(second[i][0].astype(jnp.bfloat16)))
    activated, d_pre, outputs, d_normed_two = ([], [], [], [])
    for i in images:
        pre_act = dot(gathered_two[i], up_all, ROWS_COLS) + unit_bias
        activated.append(gelu_tanh(pre_act).astype(jnp.bfloat16))
        d_act = dot(grad_rows[i], down_all, ROWS_COLS)
        d_pre.append((d_act * gelu_slope(pre_act)).astype(jnp.bfloat16))
        d_normed_two.append(scatter_dot(d_pre[i], up_all, ROWS_ROWS))
        mlp_rows = scatter_dot(activated[i], down_all, ROWS_ROWS)
        outputs.append((middle[i] + mlp_rows + biases[5]).astype(jnp.bfloat16))

    def joined(parts):
        return jnp.concatenate(parts, axis=0)

    grads_whole, units_whole = (joined(grad_rows), joined(d_pre))
    down_grad = scatter_weight(dot(grads_whole, joined(activated), COLS_COLS)).T
    up_grad = scatter_weight(dot(joined(gathered_two), units_whole, COLS_COLS))
    unit_sums = jnp.sum(units_whole, axis=0, dtype=jnp.float32)
    gain_two, shift_two, d_middle, branch = ([], [], [], [])
    for i in images:
        back, gain_part, shift_part = norm_backward(
            d_normed_two[i], second[i][1], second[i][2], norm_gains[1]
        )
        gain_two.append(gain_part)
        shift_two.append(shift_part)
        d_middle.append(cotangent[i].astype(jnp.float32) + back)
        branch.append(gather_rows(d_middle[i].astype(jnp.bfloat16)))
    d_qkv, d_normed_one = ([], [])
    for i in images:
        d_mixed = dot(branch[i], out_all, ROWS_COLS).astype(jnp.bfloat16)
        d_qkv.append(attend_backward(*saved[i], d_mixed, positions))
        d_normed_one.append(scatter_dot(d_qkv[i], qkv_all, ROWS_ROWS))
    out_grad = scatter_weight(dot(joined(branch), joined(mixed), COLS_COLS)).T
    qkv_whole = joined(d_qkv)
    qkv_grad = scatter_weight(dot(joined(gathered_one), qkv_whole, COLS_COLS))
    qkv_grad = qkv_grad.reshape(shard_rows, 3, local_cols).transpose(1, 0, 2)
    qkv_sums = jnp.sum(qkv_whole, axis=0, dtype=jnp.float32)
    input_grad, gain_one, shift_one = ([], [], [])
    for i in images:
        back, gain_part, shift_part = norm_backward(
            d_normed_one[i], first[i][1], first[i][2], norm_gains[0]
        )
        gain_one.append(gain_part)
        shift_one.append(shift_part)
        input_grad.append(d_middle[i] + back)
    blank_row = jnp.zeros((width,), jnp.float32)
    query_sums = lax.dynamic_update_slice_in_dim(blank_row, qkv_sums[:local_cols], col_start, 0)
    value_sums = lax.dynamic_update_slice_in_dim(
        blank_row, qkv_sums[2 * local_cols :], col_start, 0
    )
    unit_row = lax.dynamic_update_slice_in_dim(jnp.zeros_like(up_bias), unit_sums, unit_start, 0)
    out_sums = sum((jnp.sum(d_middle[i], axis=0) for i in images))
    top_sums = jnp.sum(cotangent, axis=(0, 1), dtype=jnp.float32)
    pieces = [
        sum(gain_one),
        sum(shift_one),
        query_sums,
        value_sums,
        sum(gain_two),
        sum(shift_two),
        out_sums,
        top_sums,
        unit_row,
    ]
    total = lax.psum(jnp.concatenate(pieces), ("fsdp", "tp"))
    rows = total[: 8 * width].reshape(8, width)
    gain_total = jnp.stack([rows[0], rows[4]])
    bias_total = jnp.stack([rows[1], rows[2], rows[3], rows[6], rows[5], rows[7]])
    return (
        jnp.stack(outputs),
        jnp.stack(input_grad),
        qkv_grad,
        out_grad,
        up_grad,
        down_grad,
        gain_total,
        bias_total,
        total[8 * width :],
    )


def solution(mesh):
    return jax.shard_map(
        per_device,
        mesh=mesh,
        in_specs=(
            P("fsdp", "tp", None),
            P(None, "fsdp", "tp"),
            P("tp", "fsdp"),
            P("fsdp", "tp"),
            P("tp", "fsdp"),
            P(),
            P(),
            P(),
            P("fsdp", "tp", None),
        ),
        out_specs=(
            P("fsdp", "tp", None),
            P("fsdp", "tp", None),
            P(None, "fsdp", "tp"),
            P("tp", "fsdp"),
            P("fsdp", "tp"),
            P("tp", "fsdp"),
            P(),
            P(),
            P(),
        ),
        check_vma=False,
    )
```

profile of v0, /device:TPU:0, one launch (start us, length us, event | category | flops | bytes accessed | tf_op | source)
XLA Modules:
  0.0 649.6 jit_solution(3423712494130585117)
XLA Ops:
  18.9 19.4 %collective-permute-done.4 = bf16[368,1152]{1,0:T(8,128)(2,1)} collective-permute-done((bf16[368,1152]{1,0:T(8,128)(2,1)S(1)}, bf16[368,1152]{1,0:T(8,128)(2,1)}, u32[]{:S(2)}, u32[]{:S(2)}) %collective-permute-start.4) | collective-permute-done | bytes 847904 | tf_op jit(solution)/shard_map/ppermute | solution.py:113
  38.4 25.5 %all-gather.5.cloned.1.call-done = bf16[1152,1728]{1,0:T(8,128)(2,1)} async-done(((bf16[72,1728]{1,0:T(8,128)(2,1)}), bf16[1152,1728]{1,0:T(8,128)(2,1)}) %all-gather.5.cloned.1.call-update) | async-done | bytes 3981328 | tf_op jit(solution)/shard_map/all_gather | solution.py:133
  93.1 9.6 %fusion.204 = (f32[8,736]{1,0:T(8,128)S(1)}, f32[8,736,736]{1,2,0:T(8,128)}) fusion(bf16[736,8,72]{0,2,1:T(8,128)(2,1)} %bitcast.205, bf16[736,8,72]{0,2,1:T(8,128)(2,1)S(1)} %bitcast.195, pred[736]{0:T(1024)(128)(4,1)S(1)} %fusion.180), kind=kOutput, calls=%fused_computation.287 | convolution fusion | flops 637028608 | bytes 19054304 | tf_op jit(solution)/shard_map/qhe,khe->hqk/dot_general | solution.py:50
  156.8 19.2 %collective-permute-done.5 = bf16[368,1152]{1,0:T(8,128)(2,1)S(1)} collective-permute-done((bf16[368,1152]{1,0:T(8,128)(2,1)S(1)}, bf16[368,1152]{1,0:T(8,128)(2,1)S(1)}, u32[]{:S(2)}, u32[]{:S(2)}) %collective-permute-start.5) | collective-permute-done | bytes 847904 | tf_op jit(solution)/shard_map/ppermute | solution.py:113
  185.5 17.8 %collective-permute-done.6 = bf16[368,1152]{1,0:T(8,128)(2,1)} collective-permute-done((bf16[368,1152]{1,0:T(8,128)(2,1)}, bf16[368,1152]{1,0:T(8,128)(2,1)}, u32[]{:S(2)}, u32[]{:S(2)}) %collective-permute-start.6) | collective-permute-done | bytes 847904 | tf_op jit(solution)/shard_map/ppermute | solution.py:113
  203.3 10.3 %fusion.112 = f32[736,2152]{1,0:T(8,128)} fusion(bf16[1152,2152]{1,0:T(8,128)(2,1)} %all-gather.9.cloned.1.call-done, bf16[368,1152]{1,0:T(8,128)(2,1)} %collective-permute-done.6, bf16[368,1152]{1,0:T(8,128)(2,1)} %get-tuple-element.94), kind=kOutput, calls=%fused_computation.155 | convolution fusion | flops 3652632576 | bytes 12989440 | tf_op jit(solution)/shard_map/dot_general | solution.py:104
  213.6 26.0 %collective-permute-done.12 = bf16[368,1152]{1,0:T(8,128)(2,1)} collective-permute-done((bf16[368,1152]{1,0:T(8,128)(2,1)S(1)}, bf16[368,1152]{1,0:T(8,128)(2,1)}, u32[]{:S(2)}, u32[]{:S(2)}) %collective-permute-start.12) | collective-permute-done | bytes 847904 | tf_op jit(solution)/shard_map/ppermute | solution.py:113
  239.6 11.1 %fusion.27 = bf16[736,2152]{1,0:T(8,128)(2,1)S(1)} fusion(bf16[1152,2152]{1,0:T(8,128)(2,1)} %all-gather.11.cloned.1.call-done, f32[736,2152]{1,0:T(8,128)} %fusion.112, f32[2152]{0:T(1024)S(1)} %dynamic_slice.17, bf16[368,1152]{1,0:T(8,128)(2,1)} %collective-permute-done.12, bf16[368,1152]{1,0:T(8,128)(2,1)S(1)} %get-tuple-element.78), kind=kOutput, calls=%fused_computation.46 | convolution fusion | flops 3684310016 | bytes 16165792 | tf_op jit(solution)/shard_map/dot_general | solution.py:104
  257.8 11.5 %multiply_convert_fusion.3 = (bf16[736,2152]{1,0:T(8,128)(2,1)}, bf16[736,2152]{1,0:T(8,128)(2,1)}, f32[736,2152]{1,0:T(8,128)}) fusion(f32[2152]{0:T(1024)S(1)} %dynamic_slice.17, f32[736,2152]{1,0:T(8,128)} %fusion.112, bf16[1152,2152]{1,0:T(8,128)(2,1)S(1)} %copy-done.73, bf16[368,1152]{1,0:T(8,128)(2,1)} %collective-permute-done.2, ...), kind=kOutput, calls=%fused_computation.52 | convolution fusion | flops 3684310016 | bytes 25669024 | tf_op jit(solution)/shard_map/dot_general | solution.py:104
  269.3 9.6 %fusion.21 = bf16[736,2152]{1,0:T(8,128)(2,1)S(1)} fusion(bf16[1152,2152]{1,0:T(8,128)(2,1)S(1)} %bitcast.236, f32[736,2152]{1,0:T(8,128)} %get-tuple-element.105, f32[2152]{0:T(1024)S(1)} %dynamic_slice.17, bf16[368,1152]{1,0:T(8,128)(2,1)} %collective-permute-done.8, bf16[368,1152]{1,0:T(8,128)(2,1)S(1)} %get-tuple-element.77), kind=kOutput, calls=%fused_computation.40 | convolution fusion | flops 3684310016 | bytes 16165792 | tf_op jit(solution)/shard_map/dot_general | solution.py:104
  284.4 14.1 %collective-permute-done.9 = bf16[368,1152]{1,0:T(8,128)(2,1)S(1)} collective-permute-done((bf16[368,1152]{1,0:T(8,128)(2,1)S(1)}, bf16[368,1152]{1,0:T(8,128)(2,1)S(1)}, u32[]{:S(2)}, u32[]{:S(2)}) %collective-permute-start.9) | collective-permute-done | bytes 847904 | tf_op jit(solution)/shard_map/ppermute | solution.py:113
  308.4 19.8 %collective-permute-done.14 = bf16[368,1152]{1,0:T(8,128)(2,1)S(1)} collective-permute-done((bf16[368,1152]{1,0:T(8,128)(2,1)S(1)}, bf16[368,1152]{1,0:T(8,128)(2,1)S(1)}, u32[]{:S(2)}, u32[]{:S(2)}) %collective-permute-start.14) | collective-permute-done | bytes 847904 | tf_op jit(solution)/shard_map/ppermute | solution.py:113
  328.2 12.6 %collective-permute-done.10 = bf16[368,1152]{1,0:T(8,128)(2,1)S(1)} collective-permute-done((bf16[368,1152]{1,0:T(8,128)(2,1)S(1)}, bf16[368,1152]{1,0:T(8,128)(2,1)S(1)}, u32[]{:S(2)}, u32[]{:S(2)}) %collective-permute-start.10) | collective-permute-done | bytes 847904 | tf_op jit(solution)/shard_map/ppermute | solution.py:113
  346.4 14.3 %convolution_convert_fusion.1 = bf16[1152,2152]{1,0:T(8,128)(2,1)} fusion(bf16[736,2152]{1,0:T(8,128)(2,1)} %copy-done.24, bf16[736,2152]{1,0:T(8,128)(2,1)} %copy-done.25, bf16[368,1152]{1,0:T(8,128)(2,1)} %collective-permute-done.6, bf16[368,1152]{1,0:T(8,128)(2,1)} %get-tuple-element.94, bf16[368,1152]{1,0:T(8,128)(2,1)} %collective-permute-done.2, ...), kind=kOutput, calls=%fused_computation.18 | convolution fusion | flops 7327198208 | bytes 14685184 | tf_op jit(solution)/shard_map/dot_general | solution.py:104
  377.7 13.0 %convolution_convert_fusion = bf16[1152,2152]{1,0:T(8,128)(2,1)} fusion(bf16[736,2152]{1,0:T(8,128)(2,1)S(1)} %copy-done.83, bf16[736,2152]{1,0:T(8,128)(2,1)S(1)} %copy-done.81, bf16[368,1152]{1,0:T(8,128)(2,1)} %collective-permute-done.12, bf16[368,1152]{1,0:T(8,128)(2,1)S(1)} %copy-done.38, bf16[368,1152]{1,0:T(8,128)(2,1)} %collective-permute-done.8, ...), kind=kOutput, calls=%fused_computation.17 | convolution fusion | flops 7327198208 | bytes 14685184 | tf_op jit(solution)/shard_map/dot_general | solution.py:104
  412.5 10.2 %fusion.161 = bf16[8,72,736]{2,1,0:T(8,128)(2,1)S(1)} fusion(bf16[736,8,72]{0,2,1:T(8,128)(2,1)S(1)} %bitcast.221, f32[8,736,736]{1,2,0:T(8,128)} %get-tuple-element.104, f32[8,736]{1,0:T(8,128)S(1)} %log_add_fusion), kind=kOutput, calls=%fused_computation.213 | convolution fusion | flops 633124864 | bytes 19053568 | tf_op jit(solution)/shard_map/hqk,qhe->khe/dot_general | solution.py:82
  422.7 12.4 %multiply_reduce_fusion = (f32[8,736]{1,0:T(8,128)S(1)}, f32[8,736,736]{1,2,0:T(8,128)}) fusion(f32[8,736,736]{1,2,0:T(8,128)} %get-tuple-element.104, f32[8,736]{1,0:T(8,128)S(1)} %log_add_fusion, bf16[736,8,72]{0,2,1:T(8,128)(2,1)S(1)} %bitcast.222, bf16[736,8,72]{0,2,1:T(8,128)(2,1)S(1)} %bitcast.218), kind=kOutput, calls=%fused_computation.1 | convolution fusion | flops 637028608 | bytes 36411392 | tf_op jit(solution)/shard_map/qhe,khe->hqk/dot_general | solution.py:77
  435.0 12.9 %multiply_convert_fusion = bf16[8,736,736]{1,2,0:T(8,128)(2,1)S(1)} fusion(f32[8,736,736]{1,2,0:T(8,128)} %get-tuple-element.110, f32[8,736,736]{1,2,0:T(8,128)} %get-tuple-element.104, f32[8,736]{1,0:T(8,128)S(1)} %get-tuple-element.109, f32[8,736]{1,0:T(8,128)S(1)} %log_add_fusion), kind=kLoop, calls=%fused_computation | loop fusion | flops 17334272 | bytes 43382784 | tf_op jit(solution)/shard_map/convert_element_type | solution.py:81
  461.1 11.6 %multiply_reduce_fusion.1 = (f32[8,736]{1,0:T(8,128)S(1)}, f32[8,736,736]{1,2,0:T(8,128)}) fusion(f32[8,736,736]{1,2,0:T(8,128)} %get-tuple-element.102, f32[8,736]{1,0:T(8,128)S(1)} %log_add_fusion.1, bf16[736,8,72]{0,2,1:T(8,128)(2,1)S(1)} %bitcast.219, bf16[736,8,72]{0,2,1:T(8,128)(2,1)S(1)} %bitcast.216), kind=kOutput, calls=%fused_computation.4 | convolution fusion | flops 637028608 | bytes 36411392 | tf_op jit(solution)/shard_map/qhe,khe->hqk/dot_general | solution.py:77
  472.7 13.0 %multiply_convert_fusion.1 = bf16[8,736,736]{1,2,0:T(8,128)(2,1)S(1)} fusion(f32[8,736,736]{1,2,0:T(8,128)} %get-tuple-element.108, f32[8,736,736]{1,2,0:T(8,128)} %get-tuple-element.102, f32[8,736]{1,0:T(8,128)S(1)} %get-tuple-element.107, f32[8,736]{1,0:T(8,128)S(1)} %log_add_fusion.1), kind=kLoop, calls=%fused_computation.3 | loop fusion | flops 17334272 | bytes 43382784 | tf_op jit(solution)/shard_map/convert_element_type | solution.py:81
  506.1 12.6 %convolution_convert_fusion.2 = bf16[1152,1728]{1,0:T(8,128)(2,1)} fusion(bf16[368,1152]{1,0:T(8,128)(2,1)} %collective-permute-done.4, bf16[368,1152]{1,0:T(8,128)(2,1)} %copy-done.45, bf16[368,1152]{1,0:T(8,128)(2,1)} %collective-permute-done, bf16[368,1152]{1,0:T(8,128)(2,1)} %copy-done.44, bf16[736,576]{0,1:T(8,128)(2,1)S(1)} %bitcast.210, ...), kind=kOutput, calls=%fused_computation.30 | convolution fusion | flops 5906571264 | bytes 12460032 | tf_op jit(solution)/shard_map/dot_general | solution.py:104
  518.7 13.3 %convert_reduce_fusion.1 = f32[1728]{0:T(1024)S(1)} fusion(bf16[736,576]{0,1:T(8,128)(2,1)} %bitcast.211, bf16[736,576]{0,1:T(8,128)(2,1)S(1)} %bitcast.201, bf16[736,576]{0,1:T(8,128)(2,1)S(1)} %bitcast.191, bf16[736,576]{0,1:T(8,128)(2,1)} %bitcast.214, bf16[736,576]{0,1:T(8,128)(2,1)S(1)} %bitcast.204, bf16[736,576]{0,1:T(8,128)(2,1)S(1)} %bitcast.194), kind=kLoop, calls=%fused_computation.19 | loop fusion | flops 33065280 | bytes 5094144 | tf_op jit(solution)/shard_map/reduce_sum | solution.py:215
  545.1 40.5 %psum.7 = f32[13520]{0:T(1024)S(1)} all-reduce(f32[13520]{0:T(1024)S(1)} %constant_dynamic-update-slice_fusion), channel_id=1, replica_groups=mesh['fsdp'=16,'tp'=2] {'fsdp','tp'}, use_global_device_ids=true, to_apply=%region_39.40 | all-reduce | flops 13520 | bytes 108160 | tf_op jit(solution)/shard_map/psum | solution.py:243
  599.3 41.2 %reduce-scatter.11.cloned.1.call-done = bf16[72,1728]{1,0:T(8,128)(2,1)} async-done(((bf16[1152,1728]{1,0:T(8,128)(2,1)}), bf16[72,1728]{1,0:T(8,128)(2,1)}) %reduce-scatter.11.cloned.1.call-update) | async-done | bytes 248848 | tf_op jit(solution)/shard_map/reduce_scatter | solution.py:137
  (337 shorter events, 232.6 us)
Async XLA Ops:
  7.2 56.7 %all-gather.5.cloned.1.call-start = ((), (), s32[]{:S(2)}) async-start(), calls=%async_computation.4 | async-start | bytes 4386816 | tf_op jit(solution)/shard_map/all_gather | solution.py:133
  9.4 112.9 %all-gather.7.cloned.1.call-start = ((), (), s32[]{:S(2)}) async-start(), calls=%async_computation.5 | async-start | bytes 1566720 | tf_op jit(solution)/shard_map/all_gather | solution.py:133
  10.2 193.1 %all-gather.9.cloned.1.call-start = ((), (), s32[]{:S(2)}) async-start(), calls=%async_computation.6 | async-start | bytes 5326848 | tf_op jit(solution)/shard_map/all_gather | solution.py:133
  10.9 228.7 %all-gather.11.cloned.1.call-start = ((), (), s32[]{:S(2)}) async-start(), calls=%async_computation.7 | async-start | bytes 5326848 | tf_op jit(solution)/shard_map/all_gather | solution.py:133
  15.5 22.8 %collective-permute-start.4 = (bf16[368,1152]{1,0:T(8,128)(2,1)S(1)}, bf16[368,1152]{1,0:T(8,128)(2,1)}, u32[]{:S(2)}, u32[]{:S(2)}) collective-permute-start(bf16[368,1152]{1,0:T(8,128)(2,1)S(1)} %get-tuple-element.70), channel_id=1, source_target_pairs={{0,1},{1,0},{2,3},{3,2},{4,5},{5,4},{6,7},{7,6},{8,9},{9,8},{10,11... | collective-permute-start | bytes 2543624 | tf_op jit(solution)/shard_map/ppermute | solution.py:113
  18.6 60.0 %collective-permute-start = (bf16[368,1152]{1,0:T(8,128)(2,1)S(1)}, bf16[368,1152]{1,0:T(8,128)(2,1)}, u32[]{:S(2)}, u32[]{:S(2)}) collective-permute-start(bf16[368,1152]{1,0:T(8,128)(2,1)S(1)} %get-tuple-element.69), channel_id=1, source_target_pairs={{0,1},{1,0},{2,3},{3,2},{4,5},{5,4},{6,7},{7,6},{8,9},{9,8},{10,11... | collective-permute-start | bytes 2543624 | tf_op jit(solution)/shard_map/ppermute | solution.py:113
  18.7 575.3 %reduce-scatter.13.cloned.1.call-start = ((), (), s32[]{:S(2)}) async-start(), calls=%async_computation.9 | async-start | bytes 1566720
  125.8 31.0 %collective-permute-start.1 = (bf16[368,1152]{1,0:T(8,128)(2,1)}, bf16[368,1152]{1,0:T(8,128)(2,1)}, u32[]{:S(2)}, u32[]{:S(2)}) collective-permute-start(bf16[368,1152]{1,0:T(8,128)(2,1)} %convolution_convert_fusion.10), channel_id=1, source_target_pairs={{0,1},{1,0},{2,3},{3,2},{4,5},{5,4},{6,7},{7,6},{8,9},{9,8},{10,11... | collective-permute-start | bytes 2543624 | tf_op jit(solution)/shard_map/ppermute | solution.py:113
  155.3 20.7 %collective-permute-start.5 = (bf16[368,1152]{1,0:T(8,128)(2,1)S(1)}, bf16[368,1152]{1,0:T(8,128)(2,1)S(1)}, u32[]{:S(2)}, u32[]{:S(2)}) collective-permute-start(bf16[368,1152]{1,0:T(8,128)(2,1)S(1)} %convolution_convert_fusion.8), channel_id=1, source_target_pairs={{0,1},{1,0},{2,3},{3,2},{4,5},{5,4},{6,7},{7,6},{8,9},{9,8},{10,11... | collective-permute-start | bytes 2543624 | tf_op jit(solution)/shard_map/ppermute | solution.py:113
  181.2 22.1 %collective-permute-start.6 = (bf16[368,1152]{1,0:T(8,128)(2,1)}, bf16[368,1152]{1,0:T(8,128)(2,1)}, u32[]{:S(2)}, u32[]{:S(2)}) collective-permute-start(bf16[368,1152]{1,0:T(8,128)(2,1)} %get-tuple-element.94), channel_id=1, source_target_pairs={{0,1},{1,0},{2,3},{3,2},{4,5},{5,4},{6,7},{7,6},{8,9},{9,8},{10,11... | collective-permute-start | bytes 2543624 | tf_op jit(solution)/shard_map/ppermute | solution.py:113
  181.9 87.4 %collective-permute-start.8 = (bf16[368,1152]{1,0:T(8,128)(2,1)S(1)}, bf16[368,1152]{1,0:T(8,128)(2,1)}, u32[]{:S(2)}, u32[]{:S(2)}) collective-permute-start(bf16[368,1152]{1,0:T(8,128)(2,1)S(1)} %get-tuple-element.77), channel_id=1, source_target_pairs={{0,1},{1,0},{2,3},{3,2},{4,5},{5,4},{6,7},{7,6},{8,9},{9,8},{10,11... | collective-permute-start | bytes 2543624 | tf_op jit(solution)/shard_map/ppermute | solution.py:113
  183.4 56.2 %collective-permute-start.12 = (bf16[368,1152]{1,0:T(8,128)(2,1)S(1)}, bf16[368,1152]{1,0:T(8,128)(2,1)}, u32[]{:S(2)}, u32[]{:S(2)}) collective-permute-start(bf16[368,1152]{1,0:T(8,128)(2,1)S(1)} %get-tuple-element.78), channel_id=1, source_target_pairs={{0,1},{1,0},{2,3},{3,2},{4,5},{5,4},{6,7},{7,6},{8,9},{9,8},{10,11... | collective-permute-start | bytes 2543624 | tf_op jit(solution)/shard_map/ppermute | solution.py:113
  184.1 73.7 %collective-permute-start.2 = (bf16[368,1152]{1,0:T(8,128)(2,1)}, bf16[368,1152]{1,0:T(8,128)(2,1)}, u32[]{:S(2)}, u32[]{:S(2)}) collective-permute-start(bf16[368,1152]{1,0:T(8,128)(2,1)} %get-tuple-element.93), channel_id=1, source_target_pairs={{0,1},{1,0},{2,3},{3,2},{4,5},{5,4},{6,7},{7,6},{8,9},{9,8},{10,11... | collective-permute-start | bytes 2543624 | tf_op jit(solution)/shard_map/ppermute | solution.py:113
  253.1 28.9 %collective-permute-start.13 = (bf16[368,1152]{1,0:T(8,128)(2,1)S(1)}, bf16[368,1152]{1,0:T(8,128)(2,1)S(1)}, u32[]{:S(2)}, u32[]{:S(2)}) collective-permute-start(bf16[368,1152]{1,0:T(8,128)(2,1)S(1)} %convolution_convert_fusion.5), channel_id=1, source_target_pairs={{0,1},{1,0},{2,3},{3,2},{4,5},{5,4},{6,7},{7,6},{8,9},{9,8},{10,11... | collective-permute-start | bytes 2543624 | tf_op jit(solution)/shard_map/ppermute | solution.py:113
  281.4 17.2 %collective-permute-start.9 = (bf16[368,1152]{1,0:T(8,128)(2,1)S(1)}, bf16[368,1152]{1,0:T(8,128)(2,1)S(1)}, u32[]{:S(2)}, u32[]{:S(2)}) collective-permute-start(bf16[368,1152]{1,0:T(8,128)(2,1)S(1)} %convolution_convert_fusion.6), channel_id=1, source_target_pairs={{0,1},{1,0},{2,3},{3,2},{4,5},{5,4},{6,7},{7,6},{8,9},{9,8},{10,11... | collective-permute-start | bytes 2543624 | tf_op jit(solution)/shard_map/ppermute | solution.py:113
  306.3 21.9 %collective-permute-start.14 = (bf16[368,1152]{1,0:T(8,128)(2,1)S(1)}, bf16[368,1152]{1,0:T(8,128)(2,1)S(1)}, u32[]{:S(2)}, u32[]{:S(2)}) collective-permute-start(bf16[368,1152]{1,0:T(8,128)(2,1)S(1)} %convert_element_type.282), channel_id=1, source_target_pairs={{0,1},{1,0},{2,3},{3,2},{4,5},{5,4},{6,7},{7,6},{8,9},{9,8},{10,11... | collective-permute-start | bytes 2543624 | tf_op jit(solution)/shard_map/ppermute | solution.py:113
  307.2 33.5 %collective-permute-start.10 = (bf16[368,1152]{1,0:T(8,128)(2,1)S(1)}, bf16[368,1152]{1,0:T(8,128)(2,1)S(1)}, u32[]{:S(2)}, u32[]{:S(2)}) collective-permute-start(bf16[368,1152]{1,0:T(8,128)(2,1)S(1)} %convert_element_type.263), channel_id=1, source_target_pairs={{0,1},{1,0},{2,3},{3,2},{4,5},{5,4},{6,7},{7,6},{8,9},{9,8},{10,11... | collective-permute-start | bytes 2543624 | tf_op jit(solution)/shard_map/ppermute | solution.py:113
  346.4 249.2 %reduce-scatter.15.cloned.1.call-start = ((), (), s32[]{:S(2)}) async-start(), calls=%async_computation.10 | async-start | bytes 5326848
  360.8 236.7 %reduce-scatter.17.cloned.1.call-start = ((), (), s32[]{:S(2)}) async-start(), calls=%async_computation.11 | async-start | bytes 5326848
  369.6 25.8 %collective-permute-start.7 = (bf16[368,1152]{1,0:T(8,128)(2,1)}, bf16[368,1152]{1,0:T(8,128)(2,1)}, u32[]{:S(2)}, u32[]{:S(2)}) collective-permute-start(bf16[368,1152]{1,0:T(8,128)(2,1)} %convolution_convert_fusion.7), channel_id=1, source_target_pairs={{0,1},{1,0},{2,3},{3,2},{4,5},{5,4},{6,7},{7,6},{8,9},{9,8},{10,11... | collective-permute-start | bytes 2543624 | tf_op jit(solution)/shard_map/ppermute | solution.py:113
  376.7 26.8 %collective-permute-start.3 = (bf16[368,1152]{1,0:T(8,128)(2,1)}, bf16[368,1152]{1,0:T(8,128)(2,1)}, u32[]{:S(2)}, u32[]{:S(2)}) collective-permute-start(bf16[368,1152]{1,0:T(8,128)(2,1)} %convolution_convert_fusion.9), channel_id=1, source_target_pairs={{0,1},{1,0},{2,3},{3,2},{4,5},{5,4},{6,7},{7,6},{8,9},{9,8},{10,11... | collective-permute-start | bytes 2543624 | tf_op jit(solution)/shard_map/ppermute | solution.py:113
  394.9 245.6 %reduce-scatter.11.cloned.1.call-start = ((), (), s32[]{:S(2)}) async-start(), calls=%async_computation.8 | async-start | bytes 4386816 | tf_op jit(solution)/shard_map/reduce_scatter | solution.py:137
  458.1 74.4 %collective-permute-start.15 = (bf16[368,1152]{1,0:T(8,128)(2,1)}, bf16[368,1152]{1,0:T(8,128)(2,1)}, u32[]{:S(2)}, u32[]{:S(2)}) collective-permute-start(bf16[368,1152]{1,0:T(8,128)(2,1)} %convolution_convert_fusion.3), channel_id=1, source_target_pairs={{0,1},{1,0},{2,3},{3,2},{4,5},{5,4},{6,7},{7,6},{8,9},{9,8},{10,11... | collective-permute-start | bytes 2543624 | tf_op jit(solution)/shard_map/ppermute | solution.py:113
  505.9 31.8 %collective-permute-start.11 = (bf16[368,1152]{1,0:T(8,128)(2,1)}, bf16[368,1152]{1,0:T(8,128)(2,1)}, u32[]{:S(2)}, u32[]{:S(2)}) collective-permute-start(bf16[368,1152]{1,0:T(8,128)(2,1)} %convolution_convert_fusion.4), channel_id=1, source_target_pairs={{0,1},{1,0},{2,3},{3,2},{4,5},{5,4},{6,7},{7,6},{8,9},{9,8},{10,11... | collective-permute-start | bytes 2543624 | tf_op jit(solution)/shard_map/ppermute | solution.py:113
  (86 other events, 1521.2 us)
Sparse Core Ops, SparseCore 0:
  10.9 52.9 all-gather.4
  66.0 37.8 all-gather.6
  106.0 53.7 all-gather.8
  161.8 53.4 all-gather.10
  346.5 56.7 reduce-scatter.12
  407.2 76.9 reduce-scatter.14
  488.8 76.9 reduce-scatter.16
  569.7 70.7 reduce-scatter.10
where the time goes:
time: 655 us; the launch traced here: 650 us
  matrix products  251 us (38%)
  waiting for transfers between devices  204 us (31%)
  other arithmetic  85 us (13%)
  blocking collectives  40.5 us (6%)
  local copies, waits for them, and re-layouts  36.1 us (6%)
  starting transfers between devices  17.3 us (3%)
  between operations  15.7 us (2%)
    dot_general x28, matrix products, dot(): lax.dot_general(left, right, (dims, ((), ())), preferred_element_type=jnp...  163 us
    ppermute x16, waiting for transfers between devices, swap_halves(): return lax.ppermute(block, 'tp', [(0, 1), (1, 0)])  135 us
    reduce_scatter x1, waiting for transfers between devices, scatter_weight(): lax.psum_scatter(whole.astype(jnp.bfloat16), 'fsdp', scatter_dimension=0,...  41.2 us
    psum x1, blocking collectives, per_device(): total = lax.psum(jnp.concatenate(pieces), ('fsdp', 'tp'))  40.5 us
    convert_element_type x2, other arithmetic, attend_backward(): d_scores = (probs_full * (d_probs - row_inner)).astype(jnp.bfloat16)  25.9 us
    all_gather x4, waiting for transfers between devices, gather_weight(): return lax.all_gather(shard, 'fsdp', axis=0, tiled=True)  25.5 us
    dot_general x2, matrix products, attend_backward(): jnp.einsum('qhe,khe->hqk', grad_heads, value_heads, preferred_element_typ...  24 us
    dot_general x2, matrix products, attend_backward(): jnp.einsum('hqk,qhe->khe', probs_full.astype(jnp.bfloat16), grad_heads, p...  19.7 us
  transfers between devices with their start and end apart: 24, of which 11 were waited for; matrix products, arithmetic and copies ran while one was open for 54% of the time, Pallas kernels for 0%

commit v1 on v0

--- a/solution.py
+++ b/solution.py
@@ -240,7 +240,9 @@
         top_sums,
         unit_row,
     ]
-    total = lax.psum(jnp.concatenate(pieces), ("fsdp", "tp"))
+    part_2 = jnp.concatenate(pieces)
+    shards = lax.all_gather(part_2, ("fsdp", "tp"), axis=0, tiled=False)
+    total = shards.sum(axis=0)
     rows = total[: 8 * width].reshape(8, width)
     gain_total = jnp.stack([rows[0], rows[4]])
     bias_total = jnp.stack([rows[1], rows[2], rows[3], rows[6], rows[5], rows[7]])

time: 655 us -> 897 us (1.37)
  waiting for transfers between devices: 204 us -> 483 us
  blocking collectives: 40.5 us -> 0 us
    unnamed x11 -> x13, waiting for transfers between devices: 1.48 us -> 264 us
    psum x1 -> x0, blocking collectives: 40.5 us -> none  [per_device(): total = lax.psum(jnp.concatenate(pieces), ('fsdp', 'tp'))]
    reduce_scatter x1, waiting for transfers between devices: 41.2 us -> 73 us  [scatter_weight(): lax.psum_scatter(whole.astype(jnp.bfloat16), 'fsdp', scatter_dimension=0,...]
    ppermute x16, waiting for transfers between devices: 135 us -> 121 us  [swap_halves(): return lax.ppermute(block, 'tp', [(0, 1), (1, 0)])]
    reduce_sum x1, other arithmetic: 13.3 us -> 23.6 us  [per_device(): qkv_sums = jnp.sum(qkv_whole, axis=0, dtype=jnp.float32)]
  transfers between devices with their start and end apart: 24 -> 25, of which waited for: 11 -> 14; matrix products, arithmetic and copies ran while one was open for 54% -> 35% of each run, Pallas kernels for 0% -> 0%
where the time goes in v1:
time: 897 us; the launch traced here: 891 us
  waiting for transfers between devices  483 us (54%)
  matrix products  245 us (27%)
  other arithmetic  92.3 us (10%)
  local copies, waits for them, and re-layouts  37.3 us (4%)
  starting transfers between devices  17.7 us (2%)
  between operations  15.5 us (2%)
    unnamed x13, waiting for transfers between devices  264 us
    dot_general x28, matrix products, dot(): lax.dot_general(left, right, (dims, ((), ())), preferred_element_type=jnp...  158 us
    ppermute x16, waiting for transfers between devices, swap_halves(): return lax.ppermute(block, 'tp', [(0, 1), (1, 0)])  121 us
    reduce_scatter x1, waiting for transfers between devices, scatter_weight(): lax.psum_scatter(whole.astype(jnp.bfloat16), 'fsdp', scatter_dimension=0,...  73 us
    all_gather x4, waiting for transfers between devices, gather_weight(): return lax.all_gather(shard, 'fsdp', axis=0, tiled=True)  25.5 us
    convert_element_type x2, other arithmetic, attend_backward(): d_scores = (probs_full * (d_probs - row_inner)).astype(jnp.bfloat16)  25.1 us
    reduce_sum x1, other arithmetic, per_device(): qkv_sums = jnp.sum(qkv_whole, axis=0, dtype=jnp.float32)  23.6 us
    dot_general x2, matrix products, attend_backward(): jnp.einsum('qhe,khe->hqk', grad_heads, value_heads, preferred_element_typ...  23.6 us
  transfers between devices with their start and end apart: 25, of which 14 were waited for; matrix products, arithmetic and copies ran while one was open for 35% of the time, Pallas kernels for 0%

profile of v1, /device:TPU:0, one launch (start us, length us, event | category | flops | bytes accessed | tf_op | source)
XLA Modules:
  0.0 891.4 jit_solution(6095487101086427059)
XLA Ops:
  18.9 19.4 %collective-permute-done.4 = bf16[368,1152]{1,0:T(8,128)(2,1)} collective-permute-done((bf16[368,1152]{1,0:T(8,128)(2,1)S(1)}, bf16[368,1152]{1,0:T(8,128)(2,1)}, u32[]{:S(2)}, u32[]{:S(2)}) %collective-permute-start.4) | collective-permute-done | bytes 847904 | tf_op jit(solution)/shard_map/ppermute | solution.py:113
  38.4 25.5 %all-gather.6.cloned.1.call-done = bf16[1152,1728]{1,0:T(8,128)(2,1)} async-done(((bf16[72,1728]{1,0:T(8,128)(2,1)}), bf16[1152,1728]{1,0:T(8,128)(2,1)}) %all-gather.6.cloned.1.call-update) | async-done | bytes 3981328 | tf_op jit(solution)/shard_map/all_gather | solution.py:133
  156.7 19.3 %collective-permute-done.5 = bf16[368,1152]{1,0:T(8,128)(2,1)S(1)} collective-permute-done((bf16[368,1152]{1,0:T(8,128)(2,1)S(1)}, bf16[368,1152]{1,0:T(8,128)(2,1)S(1)}, u32[]{:S(2)}, u32[]{:S(2)}) %collective-permute-start.5) | collective-permute-done | bytes 847904 | tf_op jit(solution)/shard_map/ppermute | solution.py:113
  186.7 16.6 %collective-permute-done.6 = bf16[368,1152]{1,0:T(8,128)(2,1)} collective-permute-done((bf16[368,1152]{1,0:T(8,128)(2,1)}, bf16[368,1152]{1,0:T(8,128)(2,1)}, u32[]{:S(2)}, u32[]{:S(2)}) %collective-permute-start.6) | collective-permute-done | bytes 847904 | tf_op jit(solution)/shard_map/ppermute | solution.py:113
  203.4 10.3 %fusion.112 = f32[736,2152]{1,0:T(8,128)} fusion(bf16[1152,2152]{1,0:T(8,128)(2,1)} %all-gather.10.cloned.1.call-done, bf16[368,1152]{1,0:T(8,128)(2,1)} %collective-permute-done.6, bf16[368,1152]{1,0:T(8,128)(2,1)} %get-tuple-element.103), kind=kOutput, calls=%fused_computation.155 | convolution fusion | flops 3652632576 | bytes 12989440 | tf_op jit(solution)/shard_map/dot_general | solution.py:104
  213.7 26.0 %collective-permute-done.12 = bf16[368,1152]{1,0:T(8,128)(2,1)} collective-permute-done((bf16[368,1152]{1,0:T(8,128)(2,1)}, bf16[368,1152]{1,0:T(8,128)(2,1)}, u32[]{:S(2)}, u32[]{:S(2)}) %collective-permute-start.12) | collective-permute-done | bytes 847904 | tf_op jit(solution)/shard_map/ppermute | solution.py:113
  239.7 11.2 %fusion.27 = bf16[736,2152]{1,0:T(8,128)(2,1)S(1)} fusion(bf16[1152,2152]{1,0:T(8,128)(2,1)} %all-gather.12.cloned.1.call-done, f32[736,2152]{1,0:T(8,128)} %fusion.112, f32[2152]{0:T(1024)S(1)} %dynamic_slice.17, bf16[368,1152]{1,0:T(8,128)(2,1)} %collective-permute-done.12, bf16[368,1152]{1,0:T(8,128)(2,1)} %get-tuple-element.87), kind=kOutput, calls=%fused_computation.46 | convolution fusion | flops 3684310016 | bytes 16165792 | tf_op jit(solution)/shard_map/dot_general | solution.py:104
  257.9 11.5 %multiply_convert_fusion.3 = (bf16[736,2152]{1,0:T(8,128)(2,1)}, bf16[736,2152]{1,0:T(8,128)(2,1)}, f32[736,2152]{1,0:T(8,128)}) fusion(f32[2152]{0:T(1024)S(1)} %dynamic_slice.17, f32[736,2152]{1,0:T(8,128)} %fusion.112, bf16[1152,2152]{1,0:T(8,128)(2,1)S(1)} %copy-done.73, bf16[368,1152]{1,0:T(8,128)(2,1)} %collective-permute-done.2, ...), kind=kOutput, calls=%fused_computation.52 | convolution fusion | flops 3684310016 | bytes 25669024 | tf_op jit(solution)/shard_map/dot_general | solution.py:104
  269.4 10.0 %fusion.21 = bf16[736,2152]{1,0:T(8,128)(2,1)S(1)} fusion(bf16[1152,2152]{1,0:T(8,128)(2,1)S(1)} %bitcast.236, f32[736,2152]{1,0:T(8,128)} %get-tuple-element.114, f32[2152]{0:T(1024)S(1)} %dynamic_slice.17, bf16[368,1152]{1,0:T(8,128)(2,1)} %collective-permute-done.8, bf16[368,1152]{1,0:T(8,128)(2,1)} %get-tuple-element.86), kind=kOutput, calls=%fused_computation.40 | convolution fusion | flops 3684310016 | bytes 16165792 | tf_op jit(solution)/shard_map/dot_general | solution.py:104
  285.0 14.2 %collective-permute-done.9 = bf16[368,1152]{1,0:T(8,128)(2,1)S(1)} collective-permute-done((bf16[368,1152]{1,0:T(8,128)(2,1)S(1)}, bf16[368,1152]{1,0:T(8,128)(2,1)S(1)}, u32[]{:S(2)}, u32[]{:S(2)}) %collective-permute-start.9) | collective-permute-done | bytes 847904 | tf_op jit(solution)/shard_map/ppermute | solution.py:113
  314.8 14.6 %collective-permute-done.14 = bf16[368,1152]{1,0:T(8,128)(2,1)} collective-permute-done((bf16[368,1152]{1,0:T(8,128)(2,1)}, bf16[368,1152]{1,0:T(8,128)(2,1)}, u32[]{:S(2)}, u32[]{:S(2)}) %collective-permute-start.14) | collective-permute-done | bytes 847904 | tf_op jit(solution)/shard_map/ppermute | solution.py:113
  332.3 11.7 %multiply_reduce_fusion = (f32[8,736]{1,0:T(8,128)S(1)}, f32[8,736,736]{1,2,0:T(8,128)}) fusion(f32[8,736,736]{1,2,0:T(8,128)} %get-tuple-element.113, f32[8,736]{1,0:T(8,128)S(1)} %log_add_fusion, bf16[736,8,72]{0,2,1:T(8,128)(2,1)S(1)} %bitcast.219, bf16[736,8,72]{0,2,1:T(8,128)(2,1)S(1)} %bitcast.218), kind=kOutput, calls=%fused_computation.1 | convolution fusion | flops 637028608 | bytes 36411392 | tf_op jit(solution)/shard_map/qhe,khe->hqk/dot_general | solution.py:77
  344.0 12.6 %multiply_convert_fusion = bf16[8,736,736]{1,2,0:T(8,128)(2,1)S(1)} fusion(f32[8,736,736]{1,2,0:T(8,128)} %get-tuple-element.119, f32[8,736,736]{1,2,0:T(8,128)} %get-tuple-element.113, f32[8,736]{1,0:T(8,128)S(1)} %get-tuple-element.118, f32[8,736]{1,0:T(8,128)S(1)} %log_add_fusion), kind=kLoop, calls=%fused_computation | loop fusion | flops 17334272 | bytes 43382784 | tf_op jit(solution)/shard_map/convert_element_type | solution.py:81
  380.6 11.8 %multiply_reduce_fusion.1 = (f32[8,736]{1,0:T(8,128)S(1)}, f32[8,736,736]{1,2,0:T(8,128)}) fusion(f32[8,736,736]{1,2,0:T(8,128)} %get-tuple-element.111, f32[8,736]{1,0:T(8,128)S(1)} %log_add_fusion.1, bf16[736,8,72]{0,2,1:T(8,128)(2,1)S(1)} %bitcast.222, bf16[736,8,72]{0,2,1:T(8,128)(2,1)S(1)} %bitcast.216), kind=kOutput, calls=%fused_computation.4 | convolution fusion | flops 637028608 | bytes 36411392 | tf_op jit(solution)/shard_map/qhe,khe->hqk/dot_general | solution.py:77
  392.5 12.6 %multiply_convert_fusion.1 = bf16[8,736,736]{1,2,0:T(8,128)(2,1)S(1)} fusion(f32[8,736,736]{1,2,0:T(8,128)} %get-tuple-element.117, f32[8,736,736]{1,2,0:T(8,128)} %get-tuple-element.111, f32[8,736]{1,0:T(8,128)S(1)} %get-tuple-element.116, f32[8,736]{1,0:T(8,128)S(1)} %log_add_fusion.1), kind=kLoop, calls=%fused_computation.3 | loop fusion | flops 17334272 | bytes 43382784 | tf_op jit(solution)/shard_map/convert_element_type | solution.py:81
  419.0 23.6 %convert_reduce_fusion.1 = f32[1728]{0:T(1024)S(1)} fusion(bf16[736,576]{0,1:T(8,128)(2,1)S(1)} %bitcast.210, bf16[736,576]{0,1:T(8,128)(2,1)S(1)} %bitcast.200, bf16[736,576]{0,1:T(8,128)(2,1)S(1)} %bitcast.190, bf16[736,576]{0,1:T(8,128)(2,1)S(1)} %bitcast.213, bf16[736,576]{0,1:T(8,128)(2,1)S(1)} %bitcast.203, bf16[736,576]{0,1:T(8,128)(2,1)S(1)} %bitcast.193), kind=kLoop, calls=%fused_computation.19 | loop fusion | flops 33065280 | bytes 5094144 | tf_op jit(solution)/shard_map/reduce_sum | solution.py:215
  460.7 14.2 %convolution_convert_fusion.1 = bf16[1152,2152]{1,0:T(8,128)(2,1)} fusion(bf16[736,2152]{1,0:T(8,128)(2,1)} %copy-done.31, bf16[736,2152]{1,0:T(8,128)(2,1)} %copy-done.32, bf16[368,1152]{1,0:T(8,128)(2,1)} %collective-permute-done.6, bf16[368,1152]{1,0:T(8,128)(2,1)} %get-tuple-element.103, bf16[368,1152]{1,0:T(8,128)(2,1)} %collective-permute-done.2, ...), kind=kOutput, calls=%fused_computation.18 | convolution fusion | flops 7327198208 | bytes 14685184 | tf_op jit(solution)/shard_map/dot_general | solution.py:104
  475.0 14.2 %convolution_convert_fusion = bf16[1152,2152]{1,0:T(8,128)(2,1)} fusion(bf16[736,2152]{1,0:T(8,128)(2,1)} %get-tuple-element.105, bf16[736,2152]{1,0:T(8,128)(2,1)} %get-tuple-element.104, bf16[368,1152]{1,0:T(8,128)(2,1)} %collective-permute-done.12, bf16[368,1152]{1,0:T(8,128)(2,1)} %get-tuple-element.87, bf16[368,1152]{1,0:T(8,128)(2,1)} %collective-permute-done.8, ...), kind=kOutput, calls=%fused_computation.17 | convolution fusion | flops 7327198208 | bytes 14685184 | tf_op jit(solution)/shard_map/dot_general | solution.py:104
  496.6 12.7 %convolution_convert_fusion.2 = bf16[1152,1728]{1,0:T(8,128)(2,1)} fusion(bf16[368,1152]{1,0:T(8,128)(2,1)} %collective-permute-done.4, bf16[368,1152]{1,0:T(8,128)(2,1)} %copy-done.42, bf16[368,1152]{1,0:T(8,128)(2,1)} %collective-permute-done, bf16[368,1152]{1,0:T(8,128)(2,1)} %copy-done.41, bf16[736,576]{0,1:T(8,128)(2,1)} %bitcast.211, ...), kind=kOutput, calls=%fused_computation.30 | convolution fusion | flops 5906571264 | bytes 12460032 | tf_op jit(solution)/shard_map/dot_general | solution.py:104
  536.8 46.2 %all-reduce.6.cloned.1.call-done = f32[432640]{0:T(1024)} async-done(((f32[432640]{0:T(1024)}), f32[432640]{0:T(1024)}) %all-reduce.6.cloned.1.call-update) | async-done | bytes 1730576
  587.6 57.6 %reduce-scatter.13.cloned.1.call-done = bf16[72,576]{1,0:T(8,128)(2,1)} async-done(((bf16[1152,576]{1,0:T(8,128)(2,1)}), bf16[72,576]{1,0:T(8,128)(2,1)}) %reduce-scatter.13.cloned.1.call-update) | async-done | bytes 82960
  646.8 79.5 %reduce-scatter.15.cloned.1.call-done = bf16[72,2152]{1,0:T(8,128)(2,1)} async-done(((bf16[1152,2152]{1,0:T(8,128)(2,1)}), bf16[72,2152]{1,0:T(8,128)(2,1)}) %reduce-scatter.15.cloned.1.call-update) | async-done | bytes 309904
  728.1 79.6 %reduce-scatter.17.cloned.1.call-done = bf16[72,2152]{1,0:T(8,128)(2,1)} async-done(((bf16[1152,2152]{1,0:T(8,128)(2,1)}), bf16[72,2152]{1,0:T(8,128)(2,1)}) %reduce-scatter.17.cloned.1.call-update) | async-done | bytes 309904
  809.6 73.0 %reduce-scatter.11.cloned.1.call-done = bf16[72,1728]{1,0:T(8,128)(2,1)} async-done(((bf16[1152,1728]{1,0:T(8,128)(2,1)}), bf16[72,1728]{1,0:T(8,128)(2,1)}) %reduce-scatter.11.cloned.1.call-update) | async-done | bytes 248848 | tf_op jit(solution)/shard_map/reduce_scatter | solution.py:137
  (336 shorter events, 247.9 us)
Async XLA Ops:
  7.2 56.7 %all-gather.6.cloned.1.call-start = ((), (), s32[]{:S(2)}) async-start(), calls=%async_computation.4 | async-start | bytes 4386816 | tf_op jit(solution)/shard_map/all_gather | solution.py:133
  9.4 112.9 %all-gather.8.cloned.1.call-start = ((), (), s32[]{:S(2)}) async-start(), calls=%async_computation.5 | async-start | bytes 1566720 | tf_op jit(solution)/shard_map/all_gather | solution.py:133
  10.2 193.2 %all-gather.10.cloned.1.call-start = ((), (), s32[]{:S(2)}) async-start(), calls=%async_computation.6 | async-start | bytes 5326848 | tf_op jit(solution)/shard_map/all_gather | solution.py:133
  10.9 228.8 %all-gather.12.cloned.1.call-start = ((), (), s32[]{:S(2)}) async-start(), calls=%async_computation.7 | async-start | bytes 5326848 | tf_op jit(solution)/shard_map/all_gather | solution.py:133
  15.5 22.8 %collective-permute-start.4 = (bf16[368,1152]{1,0:T(8,128)(2,1)S(1)}, bf16[368,1152]{1,0:T(8,128)(2,1)}, u32[]{:S(2)}, u32[]{:S(2)}) collective-permute-start(bf16[368,1152]{1,0:T(8,128)(2,1)S(1)} %get-tuple-element.79), channel_id=1, source_target_pairs={{0,1},{1,0},{2,3},{3,2},{4,5},{5,4},{6,7},{7,6},{8,9},{9,8},{10,11... | collective-permute-start | bytes 2543624 | tf_op jit(solution)/shard_map/ppermute | solution.py:113
  18.6 60.0 %collective-permute-start = (bf16[368,1152]{1,0:T(8,128)(2,1)S(1)}, bf16[368,1152]{1,0:T(8,128)(2,1)}, u32[]{:S(2)}, u32[]{:S(2)}) collective-permute-start(bf16[368,1152]{1,0:T(8,128)(2,1)S(1)} %get-tuple-element.78), channel_id=1, source_target_pairs={{0,1},{1,0},{2,3},{3,2},{4,5},{5,4},{6,7},{7,6},{8,9},{9,8},{10,11... | collective-permute-start | bytes 2543624 | tf_op jit(solution)/shard_map/ppermute | solution.py:113
  18.7 564.3 %all-reduce.6.cloned.1.call-start = ((), (), s32[]{:S(2)}) async-start(), calls=%async_computation.9 | async-start | bytes 3465216
  125.7 31.0 %collective-permute-start.1 = (bf16[368,1152]{1,0:T(8,128)(2,1)}, bf16[368,1152]{1,0:T(8,128)(2,1)}, u32[]{:S(2)}, u32[]{:S(2)}) collective-permute-start(bf16[368,1152]{1,0:T(8,128)(2,1)} %convolution_convert_fusion.10), channel_id=1, source_target_pairs={{0,1},{1,0},{2,3},{3,2},{4,5},{5,4},{6,7},{7,6},{8,9},{9,8},{10,11... | collective-permute-start | bytes 2543624 | tf_op jit(solution)/shard_map/ppermute | solution.py:113
  155.2 20.8 %collective-permute-start.5 = (bf16[368,1152]{1,0:T(8,128)(2,1)S(1)}, bf16[368,1152]{1,0:T(8,128)(2,1)S(1)}, u32[]{:S(2)}, u32[]{:S(2)}) collective-permute-start(bf16[368,1152]{1,0:T(8,128)(2,1)S(1)} %convolution_convert_fusion.8), channel_id=1, source_target_pairs={{0,1},{1,0},{2,3},{3,2},{4,5},{5,4},{6,7},{7,6},{8,9},{9,8},{10,11... | collective-permute-start | bytes 2543624 | tf_op jit(solution)/shard_map/ppermute | solution.py:113
  181.3 22.1 %collective-permute-start.6 = (bf16[368,1152]{1,0:T(8,128)(2,1)}, bf16[368,1152]{1,0:T(8,128)(2,1)}, u32[]{:S(2)}, u32[]{:S(2)}) collective-permute-start(bf16[368,1152]{1,0:T(8,128)(2,1)} %get-tuple-element.103), channel_id=1, source_target_pairs={{0,1},{1,0},{2,3},{3,2},{4,5},{5,4},{6,7},{7,6},{8,9},{9,8},{10,11... | collective-permute-start | bytes 2543624 | tf_op jit(solution)/shard_map/ppermute | solution.py:113
  183.1 86.3 %collective-permute-start.8 = (bf16[368,1152]{1,0:T(8,128)(2,1)}, bf16[368,1152]{1,0:T(8,128)(2,1)}, u32[]{:S(2)}, u32[]{:S(2)}) collective-permute-start(bf16[368,1152]{1,0:T(8,128)(2,1)} %get-tuple-element.86), channel_id=1, source_target_pairs={{0,1},{1,0},{2,3},{3,2},{4,5},{5,4},{6,7},{7,6},{8,9},{9,8},{10,11... | collective-permute-start | bytes 2543624 | tf_op jit(solution)/shard_map/ppermute | solution.py:113
  184.6 55.1 %collective-permute-start.12 = (bf16[368,1152]{1,0:T(8,128)(2,1)}, bf16[368,1152]{1,0:T(8,128)(2,1)}, u32[]{:S(2)}, u32[]{:S(2)}) collective-permute-start(bf16[368,1152]{1,0:T(8,128)(2,1)} %get-tuple-element.87), channel_id=1, source_target_pairs={{0,1},{1,0},{2,3},{3,2},{4,5},{5,4},{6,7},{7,6},{8,9},{9,8},{10,11... | collective-permute-start | bytes 2543624 | tf_op jit(solution)/shard_map/ppermute | solution.py:113
  185.2 72.6 %collective-permute-start.2 = (bf16[368,1152]{1,0:T(8,128)(2,1)}, bf16[368,1152]{1,0:T(8,128)(2,1)}, u32[]{:S(2)}, u32[]{:S(2)}) collective-permute-start(bf16[368,1152]{1,0:T(8,128)(2,1)} %get-tuple-element.102), channel_id=1, source_target_pairs={{0,1},{1,0},{2,3},{3,2},{4,5},{5,4},{6,7},{7,6},{8,9},{9,8},{10,11... | collective-permute-start | bytes 2543624 | tf_op jit(solution)/shard_map/ppermute | solution.py:113
  253.5 29.0 %collective-permute-start.13 = (bf16[368,1152]{1,0:T(8,128)(2,1)S(1)}, bf16[368,1152]{1,0:T(8,128)(2,1)S(1)}, u32[]{:S(2)}, u32[]{:S(2)}) collective-permute-start(bf16[368,1152]{1,0:T(8,128)(2,1)S(1)} %convolution_convert_fusion.5), channel_id=1, source_target_pairs={{0,1},{1,0},{2,3},{3,2},{4,5},{5,4},{6,7},{7,6},{8,9},{9,8},{10,11... | collective-permute-start | bytes 2543624 | tf_op jit(solution)/shard_map/ppermute | solution.py:113
  281.9 17.3 %collective-permute-start.9 = (bf16[368,1152]{1,0:T(8,128)(2,1)S(1)}, bf16[368,1152]{1,0:T(8,128)(2,1)S(1)}, u32[]{:S(2)}, u32[]{:S(2)}) collective-permute-start(bf16[368,1152]{1,0:T(8,128)(2,1)S(1)} %convolution_convert_fusion.6), channel_id=1, source_target_pairs={{0,1},{1,0},{2,3},{3,2},{4,5},{5,4},{6,7},{7,6},{8,9},{9,8},{10,11... | collective-permute-start | bytes 2543624 | tf_op jit(solution)/shard_map/ppermute | solution.py:113
  307.3 22.1 %collective-permute-start.14 = (bf16[368,1152]{1,0:T(8,128)(2,1)}, bf16[368,1152]{1,0:T(8,128)(2,1)}, u32[]{:S(2)}, u32[]{:S(2)}) collective-permute-start(bf16[368,1152]{1,0:T(8,128)(2,1)} %convert_element_type.282), channel_id=1, source_target_pairs={{0,1},{1,0},{2,3},{3,2},{4,5},{5,4},{6,7},{7,6},{8,9},{9,8},{10,11... | collective-permute-start | bytes 2543624 | tf_op jit(solution)/shard_map/ppermute | solution.py:113
  313.4 56.7 %collective-permute-start.10 = (bf16[368,1152]{1,0:T(8,128)(2,1)S(1)}, bf16[368,1152]{1,0:T(8,128)(2,1)S(1)}, u32[]{:S(2)}, u32[]{:S(2)}) collective-permute-start(bf16[368,1152]{1,0:T(8,128)(2,1)S(1)} %convert_element_type.263), channel_id=1, source_target_pairs={{0,1},{1,0},{2,3},{3,2},{4,5},{5,4},{6,7},{7,6},{8,9},{9,8},{10,11... | collective-permute-start | bytes 2543624 | tf_op jit(solution)/shard_map/ppermute | solution.py:113
  414.1 28.9 %collective-permute-start.15 = (bf16[368,1152]{1,0:T(8,128)(2,1)S(1)}, bf16[368,1152]{1,0:T(8,128)(2,1)S(1)}, u32[]{:S(2)}, u32[]{:S(2)}) collective-permute-start(bf16[368,1152]{1,0:T(8,128)(2,1)S(1)} %convolution_convert_fusion.3), channel_id=1, source_target_pairs={{0,1},{1,0},{2,3},{3,2},{4,5},{5,4},{6,7},{7,6},{8,9},{9,8},{10,11... | collective-permute-start | bytes 2543624 | tf_op jit(solution)/shard_map/ppermute | solution.py:113
  417.6 27.6 %collective-permute-start.11 = (bf16[368,1152]{1,0:T(8,128)(2,1)S(1)}, bf16[368,1152]{1,0:T(8,128)(2,1)S(1)}, u32[]{:S(2)}, u32[]{:S(2)}) collective-permute-start(bf16[368,1152]{1,0:T(8,128)(2,1)S(1)} %convolution_convert_fusion.4), channel_id=1, source_target_pairs={{0,1},{1,0},{2,3},{3,2},{4,5},{5,4},{6,7},{7,6},{8,9},{9,8},{10,11... | collective-permute-start | bytes 2543624 | tf_op jit(solution)/shard_map/ppermute | solution.py:113
  453.3 191.9 %reduce-scatter.13.cloned.1.call-start = ((), (), s32[]{:S(2)}) async-start(), calls=%async_computation.10 | async-start | bytes 1566720
  460.5 265.8 %reduce-scatter.15.cloned.1.call-start = ((), (), s32[]{:S(2)}) async-start(), calls=%async_computation.11 | async-start | bytes 5326848
  474.9 332.8 %reduce-scatter.17.cloned.1.call-start = ((), (), s32[]{:S(2)}) async-start(), calls=%async_computation.12 | async-start | bytes 5326848
  489.2 393.4 %reduce-scatter.11.cloned.1.call-start = ((), (), s32[]{:S(2)}) async-start(), calls=%async_computation.8 | async-start | bytes 4386816 | tf_op jit(solution)/shard_map/reduce_scatter | solution.py:137
  495.9 20.3 %collective-permute-start.7 = (bf16[368,1152]{1,0:T(8,128)(2,1)}, bf16[368,1152]{1,0:T(8,128)(2,1)}, u32[]{:S(2)}, u32[]{:S(2)}) collective-permute-start(bf16[368,1152]{1,0:T(8,128)(2,1)} %convolution_convert_fusion.7), channel_id=1, source_target_pairs={{0,1},{1,0},{2,3},{3,2},{4,5},{5,4},{6,7},{7,6},{8,9},{9,8},{10,11... | collective-permute-start | bytes 2543624 | tf_op jit(solution)/shard_map/ppermute | solution.py:113
  (83 other events, 1347.1 us)
Sparse Core Ops, SparseCore 0:
  10.9 52.9 all-gather.5
  66.0 37.8 all-gather.7
  106.0 53.6 all-gather.9
  161.7 53.5 all-gather.11
  453.4 129.5 all-reduce.5
  586.6 58.5 reduce-scatter.12
  649.2 76.9 reduce-scatter.14
  730.8 76.8 reduce-scatter.16
  811.7 70.8 reduce-scatter.10
